TPU v7x, 256 devices: a whole 4x4x8 slice. The times are simulated.
256 devices in a mesh: section: 32 (over z, x), dp: 4 (over y), expert: 2 (over core).
Axes of the slice: x: 4, y: 4, z: 8, core: 2. Of those that a mesh axis runs over, the one named last changes fastest.
Arguments:
- tokens: bfloat16 [32768, 1024], P(('section', 'dp', 'expert')), may hold values from -6 to 6
- expert_ids: int32 [32768, 8], P(('section', 'dp', 'expert')), may hold values from 0 to 31, all different within a row; in each aligned block of 128 rows (0 to 127, 128 to 255, ...) at most 40 rows name the same one
- probs: float32 [32768, 8], P(('section', 'dp', 'expert')), may hold values from 0.1 to 1
- first_weight: bfloat16 [32, 1024, 512], P('section'), may hold values from -0.1875 to 0.1875
- second_weight: bfloat16 [32, 512, 1024], P('section'), may hold values from -0.375 to 0.375
- upstream: bfloat16 [32768, 1024], P(('section', 'dp', 'expert')), may hold values from -6 to 6
Outputs:
- mixed: bfloat16 [32768, 1024], P(('section', 'dp', 'expert'))
- input_grad: bfloat16 [32768, 1024], P(('section', 'dp', 'expert'))
- second_grad: bfloat16 [32, 512, 1024], P('section', ('dp', 'expert'))
- prob_grad: float32 [32768, 8], P(('section', 'dp', 'expert'))
Inputs may be any that keep to these rules, and one draw needn't show every extreme that they name: `expert_ids`: in each aligned block of 128 rows (one group's tokens), no expert is named by more than 40 rows, and in some block one expert is named by exactly 40 rows. The 8 experts of a row differ, and every expert is named somewhere.
All inputs are finite; a program needn't handle non-finite values.
Results may differ from a plain program's by a relative error of at most 0.0064.
Values may be sent and summed in bfloat16 or wider, within the bound.
A program may use at most 128 MiB of HBM per device.

v0:
```python
import jax
import jax.numpy as jnp
from jax import lax
from jax.sharding import PartitionSpec as P

EXPERTS = 32
TOPK = 8
SLOT_CAPACITY = 40


def silu_grad(value):
    sig = jax.nn.sigmoid(value)
    return sig * (1.0 + value * (1.0 - sig))


def body(tokens, expert_ids, probs, first_weight, second_weight, upstream):
    sections = lax.axis_size("section")
    local_experts = first_weight.shape[0]
    tok_rows = tokens.shape[0]
    row_width = tokens.shape[1]
    flat_ids = expert_ids.reshape(-1)
    onehot = (flat_ids[:, None] == jnp.arange(EXPERTS, dtype=jnp.int32)[None, :]).astype(jnp.int32)
    before = jnp.cumsum(onehot, axis=0) - onehot
    slot_pos = jnp.sum(before * onehot, axis=1)
    slot_index = flat_ids * SLOT_CAPACITY + slot_pos

    def place_rows(values):
        filled = (
            jnp.zeros((EXPERTS * SLOT_CAPACITY, row_width), values.dtype).at[slot_index].set(values)
        )
        return filled.reshape(sections, local_experts, SLOT_CAPACITY, row_width)

    token_slots = place_rows(jnp.repeat(tokens, TOPK, axis=0))
    up_float = upstream.astype(jnp.float32)
    scaled = (
        (probs[:, :, None] * up_float[:, None, :])
        .astype(jnp.bfloat16)
        .reshape(tok_rows * TOPK, row_width)
    )
    arrived = lax.all_to_all(token_slots, "section", split_axis=0, concat_axis=2, tiled=True)
    input_slot_buffer = arrived.reshape(local_experts, sections * SLOT_CAPACITY, row_width)
    pre_act = jnp.einsum(
        "erd,edf->erf", input_slot_buffer, first_weight, preferred_element_type=jnp.float32
    )
    hidden = jax.nn.silu(pre_act).astype(jnp.bfloat16)
    expert_out = jnp.einsum(
        "erf,efd->erd", hidden, second_weight, preferred_element_type=jnp.float32
    ).astype(jnp.bfloat16)
    returned = lax.all_to_all(
        expert_out.reshape(1, local_experts, sections * SLOT_CAPACITY, row_width),
        "section",
        split_axis=2,
        concat_axis=0,
        tiled=True,
    )
    picked = (
        returned.reshape(EXPERTS * SLOT_CAPACITY, row_width)[slot_index]
        .astype(jnp.float32)
        .reshape(tok_rows, TOPK, row_width)
    )
    mixed = jnp.sum(probs[:, :, None] * picked, axis=1).astype(jnp.bfloat16)
    prob_grad = jnp.sum(up_float[:, None, :] * picked, axis=2)
    grad_arrived = lax.all_to_all(
        place_rows(scaled), "section", split_axis=0, concat_axis=2, tiled=True
    )
    gradient_buffer = grad_arrived.reshape(local_experts, sections * SLOT_CAPACITY, row_width)
    shares = lax.psum_scatter(
        jnp.einsum("erf,erd->fed", hidden, gradient_buffer, preferred_element_type=jnp.float32),
        ("dp", "expert"),
        scatter_dimension=0,
        tiled=True,
    )
    second_grad = shares.transpose(1, 0, 2).astype(jnp.bfloat16)
    hid_grad = jnp.einsum(
        "erd,efd->erf", gradient_buffer, second_weight, preferred_element_type=jnp.float32
    )
    pre_grad = (hid_grad * silu_grad(pre_act)).astype(jnp.bfloat16)
    input_rows = jnp.einsum(
        "erf,edf->erd", pre_grad, first_weight, preferred_element_type=jnp.float32
    ).astype(jnp.bfloat16)
    grad_back = lax.all_to_all(
        input_rows.reshape(1, local_experts, sections * SLOT_CAPACITY, row_width),
        "section",
        split_axis=2,
        concat_axis=0,
        tiled=True,
    )
    gathered = (
        grad_back.reshape(EXPERTS * SLOT_CAPACITY, row_width)[slot_index]
        .astype(jnp.float32)
        .reshape(tok_rows, TOPK, row_width)
    )
    input_grad = jnp.sum(gathered, axis=1).astype(jnp.bfloat16)
    return (mixed, input_grad, second_grad, prob_grad)


def solution(mesh):
    return jax.shard_map(
        body,
        mesh=mesh,
        in_specs=(
            P(("section", "dp", "expert"), None),
            P(("section", "dp", "expert"), None),
            P(("section", "dp", "expert"), None),
            P("section", None, None),
            P("section", None, None),
            P(("section", "dp", "expert"), None),
        ),
        out_specs=(
            P(("section", "dp", "expert"), None),
            P(("section", "dp", "expert"), None),
            P("section", ("dp", "expert"), None),
            P(("section", "dp", "expert"), None),
        ),
        check_vma=False,
    )
```

profile of v0, /device:TPU:2, one launch (start us, length us, event | category | flops | bytes accessed | tf_op | source)
XLA Modules:
  0.0 468.6 jit_solution(13929625554885568245)
XLA Ops:
  2.6 9.0 %reduce-window.6 = s32[32,8,128]{2,1,0:T(8,128)S(1)} reduce-window(s32[32,8,128]{2,1,0:T(8,128)S(1)} %fusion.25, s32[]{:T(128)} %constant.5.clone.1), window={size=1x1x128 pad=0_0x0_0x127_0}, to_apply=%region_0.0 | reduce-window | flops 4161536 | bytes 262148 | tf_op jit(solution)/shard_map/reduce-window
  12.1 7.5 %scatter_custom_fusion = bf16[1280,1024]{1,0:T(8,128)(2,1)} fusion(s32[1024]{0:T(1024)S(1)} %bitcast.92, bf16[]{:T(256)} %constant.6.clone.1, bf16[128,1024]{1,0:T(8,128)(2,1)} %param.6), kind=kCustom, calls=%fused_computation.22 | custom fusion | bytes 2883586 | tf_op jit(solution)/shard_map/scatter | solution.py:29
  19.6 11.8 %all-to-all-start = ((bf16[32,1,40,1024]{3,2,1,0:T(8,128)(2,1)}), bf16[32,1,40,1024]{3,2,1,0:T(8,128)(2,1)}, u32[]{:S(2)}, u32[]{:S(2)}) async-start(bf16[32,1,40,1024]{3,2,1,0:T(8,128)(2,1)} %bitcast.87), calls=%async_computation | async-start | bytes 5242880 | tf_op jit(solution)/shard_map/all_to_all | solution.py:40
  31.7 7.5 %scatter_custom_fusion.1 = bf16[1280,1024]{1,0:T(8,128)(2,1)} fusion(s32[1024]{0:T(1024)S(1)} %bitcast.93, f32[128,1024]{1,0:T(8,128)S(1)} %convert_element_type.68, f32[1024]{0:T(1024)S(1)} %mul.79, bf16[]{:T(256)} %constant.6.clone.1), kind=kCustom, calls=%fused_computation.20 | custom fusion | flops 2097152 | bytes 3149826 | tf_op jit(solution)/shard_map/scatter | solution.py:29
  39.2 52.3 %all-to-all-done = bf16[32,1,40,1024]{3,2,1,0:T(8,128)(2,1)} async-done(((bf16[32,1,40,1024]{3,2,1,0:T(8,128)(2,1)}), bf16[32,1,40,1024]{3,2,1,0:T(8,128)(2,1)}, u32[]{:S(2)}, u32[]{:S(2)}) %all-to-all-start) | async-done | bytes 2621472 | tf_op jit(solution)/shard_map/all_to_all | solution.py:40
  91.5 7.9 %all-to-all-start.2 = ((bf16[32,1,40,1024]{3,2,1,0:T(8,128)(2,1)}), bf16[32,1,40,1024]{3,2,1,0:T(8,128)(2,1)}, u32[]{:S(2)}, u32[]{:S(2)}) async-start(bf16[32,1,40,1024]{3,2,1,0:T(8,128)(2,1)} %bitcast.86), calls=%async_computation.2 | async-start | bytes 5242880 | tf_op jit(solution)/shard_map/all_to_all | solution.py:63
  104.3 18.2 %copy.58 = bf16[1,1,1280,1024]{3,1,0,2:T(2,128)(2,1)} copy(bf16[1,1,1280,1024]{3,2,1,0:T(8,128)(2,1)S(1)} %fusion.3) | data formatting | bytes 5242880 | tf_op jit(solution)/shard_map/reshape | solution.py:50
  123.1 17.0 %reduce.5 = bf16[1280,1024]{1,0:T(8,128)(2,1)} reduce(bf16[1280,1,1,1024]{3,2,1,0:T(2,128)(2,1)} %bitcast.82, bf16[]{:T(256)} %broadcast.78), dimensions={1,2}, to_apply=%bitcast.77.reduce_sub_computation | reduce | bytes 5242882
  140.1 7.7 %reshape.222 = bf16[32,2,20480]{2,1,0:T(2,128)(2,1)} reshape(bf16[1280,1024]{1,0:T(8,128)(2,1)} %reduce.5) | data formatting | bytes 5242880
  147.8 11.0 %all-to-all-done.2 = bf16[32,1,40,1024]{3,2,1,0:T(8,128)(2,1)} async-done(((bf16[32,1,40,1024]{3,2,1,0:T(8,128)(2,1)}), bf16[32,1,40,1024]{3,2,1,0:T(8,128)(2,1)}, u32[]{:S(2)}, u32[]{:S(2)}) %all-to-all-start.2) | async-done | bytes 2621472 | tf_op jit(solution)/shard_map/all_to_all | solution.py:63
  158.8 7.7 %all-to-all-start.1 = ((bf16[32,2,20480]{2,1,0:T(2,128)(2,1)}), bf16[32,2,20480]{2,1,0:T(2,128)(2,1)}, u32[]{:S(2)}, u32[]{:S(2)}) async-start(bf16[32,2,20480]{2,1,0:T(2,128)(2,1)} %reshape.222), calls=%async_computation.1 | async-start | bytes 5242880 | tf_op jit(solution)/shard_map/all_to_all | solution.py:49
  166.5 7.3 %fusion.4 = bf16[1,1,1280,1024]{3,2,1,0:T(8,128)(2,1)} fusion(bf16[1280,1024]{1,0:T(8,128)(2,1)} %bitcast.13, f32[1280,512]{1,0:T(8,128)} %copy-done.8, bf16[1,512,1024]{2,1,0:T(8,128)(2,1)S(1)} %copy-done, bf16[1,1024,512]{2,1,0:T(8,128)(2,1)S(1)} %copy-done.6), kind=kOutput, calls=%fused_computation.14 | convolution fusion | flops 2691563520 | bytes 9961472 | tf_op jit(solution)/shard_map/erf,edf->erd/dot_general | solution.py:78
  173.9 6.0 %copy.57 = bf16[1,1,1280,1024]{3,1,0,2:T(2,128)(2,1)} copy(bf16[1,1,1280,1024]{3,2,1,0:T(8,128)(2,1)} %fusion.4) | data formatting | bytes 5242880 | tf_op jit(solution)/shard_map/reshape | solution.py:82
  179.8 17.0 %reduce.6 = bf16[1280,1024]{1,0:T(8,128)(2,1)} reduce(bf16[1280,1,1,1024]{3,2,1,0:T(2,128)(2,1)} %bitcast.83, bf16[]{:T(256)} %broadcast.78), dimensions={1,2}, to_apply=%bitcast.76.reduce_sub_computation | reduce | bytes 5242882
  196.8 7.7 %reshape.224 = bf16[32,2,20480]{2,1,0:T(2,128)(2,1)} reshape(bf16[1280,1024]{1,0:T(8,128)(2,1)} %reduce.6) | data formatting | bytes 5242880
  204.5 21.1 %all-to-all-done.1 = bf16[32,2,20480]{2,1,0:T(2,128)(2,1)} async-done(((bf16[32,2,20480]{2,1,0:T(2,128)(2,1)}), bf16[32,2,20480]{2,1,0:T(2,128)(2,1)}, u32[]{:S(2)}, u32[]{:S(2)}) %all-to-all-start.1) | async-done | bytes 2621472 | tf_op jit(solution)/shard_map/all_to_all | solution.py:49
  225.6 6.5 %all-to-all-start.3 = ((bf16[32,2,20480]{2,1,0:T(2,128)(2,1)}), bf16[32,2,20480]{2,1,0:T(2,128)(2,1)}, u32[]{:S(2)}, u32[]{:S(2)}) async-start(bf16[32,2,20480]{2,1,0:T(2,128)(2,1)} %reshape.224), calls=%async_computation.3 | async-start | bytes 5242880 | tf_op jit(solution)/shard_map/all_to_all | solution.py:81
  233.4 5.5 %convolution_bitcast_fusion = f32[512,1,1024]{0,2,1:T(8,128)} fusion(bf16[1280,1024]{1,0:T(8,128)(2,1)} %bitcast.13, f32[1280,512]{1,0:T(8,128)} %copy-done.8), kind=kOutput, calls=%fused_computation.26 | convolution fusion | flops 1345454080 | bytes 7340032 | tf_op jit(solution)/shard_map/erf,erd->fed/dot_general | solution.py:68
  243.7 171.5 %all-reduce.2 = bf16[512,1,1024]{2,1,0:T(2,128)(2,1)} all-reduce(f32[512,1,1024]{2,1,0:T(1,128)S(1)} %copy.40), channel_id=2, replica_groups=mesh['section'=32,'dp'=4,'expert'=2] {'dp','expert'}, use_global_device_ids=true, to_apply=%region_7.8.clone | all-reduce | flops 524288 | bytes 3145728
  417.1 10.9 %reshape.223 = bf16[1280,1,1,1024]{3,2,1,0:T(2,128)(2,1)} reshape(bf16[32,2,20480]{2,1,0:T(2,128)(2,1)} %all-to-all-done.1) | data formatting | bytes 5242880
  433.1 7.1 %gather_fusion = bf16[1024,1024]{1,0:T(8,128)(2,1)S(1)} fusion(bf16[1280,1024]{1,0:T(8,128)(2,1)} %bitcast.81, s32[1024]{0:T(1024)S(1)} %broadcast_clamp_fusion), kind=kCustom, calls=%fused_computation | custom fusion | bytes 4198400 | tf_op jit(solution)/shard_map/gather | solution.py:57
  443.2 10.9 %reshape.225 = bf16[1280,1,1,1024]{3,2,1,0:T(2,128)(2,1)} reshape(bf16[32,2,20480]{2,1,0:T(2,128)(2,1)} %all-to-all-done.3) | data formatting | bytes 5242880
  454.1 5.0 %copy.54 = bf16[1,1,1280,1024]{3,2,0,1:T(8,128)(2,1)} copy(bf16[1,1,1280,1024]{3,1,0,2:T(2,128)(2,1)} %bitcast.85) | data formatting | bytes 5242880
  459.1 7.1 %gather_fusion.1 = bf16[1024,1024]{1,0:T(8,128)(2,1)S(1)} fusion(bf16[1280,1024]{1,0:T(8,128)(2,1)} %bitcast.80, s32[1024]{0:T(1024)S(1)} %broadcast_clamp_fusion), kind=kCustom, calls=%fused_computation.1 | custom fusion | bytes 4198400 | tf_op jit(solution)/shard_map/gather | solution.py:89
  (49 shorter events, 25.5 us)
Async XLA Ops:
  0.6 102.1 %copy-start = (bf16[1,512,1024]{2,1,0:T(8,128)(2,1)S(1)}, bf16[1,512,1024]{2,1,0:T(8,128)(2,1)}, u32[]{:S(2)}) copy-start(bf16[1,512,1024]{2,1,0:T(8,128)(2,1)} %param.10) | copy-start | bytes 3145732
  19.6 11.8 %copy-start.5 = (f32[128,8]{0,1:T(8,128)S(1)}, f32[128,8]{0,1:T(8,128)}, u32[]{:S(2)}) copy-start(f32[128,8]{0,1:T(8,128)} %param.8) | copy-start | bytes 12292
  19.6 12.0 %copy-start.4 = (bf16[128,1024]{1,0:T(8,128)(2,1)S(1)}, bf16[128,1024]{1,0:T(8,128)(2,1)}, u32[]{:S(2)}) copy-start(bf16[128,1024]{1,0:T(8,128)(2,1)} %param.11) | copy-start | bytes 786436
  19.6 71.9 %all-to-all-start = ((bf16[32,1,40,1024]{3,2,1,0:T(8,128)(2,1)}), bf16[32,1,40,1024]{3,2,1,0:T(8,128)(2,1)}, u32[]{:S(2)}, u32[]{:S(2)}) async-start(bf16[32,1,40,1024]{3,2,1,0:T(8,128)(2,1)} %bitcast.87), calls=%async_computation | async-start | bytes 5242880 | tf_op jit(solution)/shard_map/all_to_all | solution.py:40
  31.7 59.9 %copy-start.2 = (f32[128,1024]{1,0:T(8,128)}, f32[128,1024]{1,0:T(8,128)S(1)}, u32[]{:S(2)}) copy-start(f32[128,1024]{1,0:T(8,128)S(1)} %convert_element_type.68) | copy-start | bytes 1572868
  91.5 7.9 %copy-start.6 = (bf16[1,1024,512]{2,1,0:T(8,128)(2,1)S(1)}, bf16[1,1024,512]{2,1,0:T(8,128)(2,1)}, u32[]{:S(2)}) copy-start(bf16[1,1024,512]{2,1,0:T(8,128)(2,1)} %param.9) | copy-start | bytes 3145732
  91.5 67.2 %all-to-all-start.2 = ((bf16[32,1,40,1024]{3,2,1,0:T(8,128)(2,1)}), bf16[32,1,40,1024]{3,2,1,0:T(8,128)(2,1)}, u32[]{:S(2)}, u32[]{:S(2)}) async-start(bf16[32,1,40,1024]{3,2,1,0:T(8,128)(2,1)} %bitcast.86), calls=%async_computation.2 | async-start | bytes 5242880 | tf_op jit(solution)/shard_map/all_to_all | solution.py:63
  102.7 1.6 copy-start.8
  158.8 66.8 %all-to-all-start.1 = ((bf16[32,2,20480]{2,1,0:T(2,128)(2,1)}), bf16[32,2,20480]{2,1,0:T(2,128)(2,1)}, u32[]{:S(2)}, u32[]{:S(2)}) async-start(bf16[32,2,20480]{2,1,0:T(2,128)(2,1)} %reshape.222), calls=%async_computation.1 | async-start | bytes 5242880 | tf_op jit(solution)/shard_map/all_to_all | solution.py:49
  204.5 27.6 %copy-start.7 = (u32[256]{0:T(256)S(1)}, u32[256]{0:T(256)}, u32[]{:S(2)}) copy-start(u32[256]{0:T(256)} %constant.28) | copy-start | bytes 3076
  225.6 217.6 %all-to-all-start.3 = ((bf16[32,2,20480]{2,1,0:T(2,128)(2,1)}), bf16[32,2,20480]{2,1,0:T(2,128)(2,1)}, u32[]{:S(2)}, u32[]{:S(2)}) async-start(bf16[32,2,20480]{2,1,0:T(2,128)(2,1)} %reshape.224), calls=%async_computation.3 | async-start | bytes 5242880 | tf_op jit(solution)/shard_map/all_to_all | solution.py:81
  433.0 7.1 %copy-start.3 = (f32[128,1024]{1,0:T(8,128)S(1)}, f32[128,1024]{1,0:T(8,128)}, u32[]{:S(2)}) copy-start(f32[128,1024]{1,0:T(8,128)} %copy-done.2) | copy-start | bytes 1572868
  459.1 9.3 %copy-start.1 = (bf16[1,512,1024]{2,1,0:T(8,128)(2,1)S(1)}, bf16[1,512,1024]{2,1,0:T(8,128)(2,1)}, u32[]{:S(2)}) copy-start(bf16[1,512,1024]{2,1,0:T(8,128)(2,1)} %param.10) | copy-start | bytes 3145732
where the time goes:
time: 478 us; the launch traced here: 469 us
  blocking collectives  171 us (36%)
  local copies, waits for them, and re-layouts  103 us (22%)
  waiting for transfers between devices  84.4 us (18%)
  other arithmetic  56 us (12%)
  starting transfers between devices  33.9 us (7%)
  matrix products  17.7 us (4%)
    unnamed x1, blocking collectives  171 us
    all_to_all x1, waiting for transfers between devices, body(): lax.all_to_all(token_slots, 'section', split_axis=0, concat_axis=2, tiled...  52.3 us
    unnamed x30, local copies, waits for them, and re-layouts  51.2 us
    unnamed x2, other arithmetic  34 us
    all_to_all x1, waiting for transfers between devices, body(): lax.all_to_all(expert_out.reshape(1, local_experts, sections * SLOT_CAPAC...  21.1 us
    reshape x1, local copies, waits for them, and re-layouts, body(): expert_out.reshape(1, local_experts, sections * SLOT_CAPACITY, row_width)  18.2 us
    all_to_all x1, starting transfers between devices, body(): lax.all_to_all(token_slots, 'section', split_axis=0, concat_axis=2, tiled...  11.8 us
    all_to_all x1, waiting for transfers between devices, body(): lax.all_to_all(place_rows(scaled), 'section', split_axis=0, concat_axis=2...  11 us
  transfers between devices with their start and end apart: 4, of which 3 were waited for; matrix products, arithmetic and copies ran while one was open for 28% of the time, Pallas kernels for 0%

commit v1 on v0

v1 whole, which is shorter than its diff:
```python
import jax
import jax.numpy as jnp
from jax import lax
from jax.experimental import pallas as pl
from jax.experimental.pallas import tpu as pltpu
from jax.sharding import PartitionSpec as P

MESH = pl.DeviceIdType.MESH
F32 = jnp.float32
BF16 = jnp.bfloat16

NZ, NX, NY = 8, 4, 4
TOK = 128
D = 1024
FF = 512
TOPK = 8
HALF = D // 2
ROWS = NZ * TOK
BLOCK = 2 * TOK
NN = (((1,), (0,)), ((), ()))
NT = (((1,), (1,)), ((), ()))
TN = (((0,), (0,)), ((), ()))


def slot_of(offset):
    offset = offset % NZ
    if offset > NZ // 2:
        return 2 * (NZ - offset)
    return 2 * offset - 1 if offset else 0


def kernel(
    tok_in, up_in, w1_in, w2_in, ids, probs,
    mixed, igrad, sgrad, pgrad,
    tu, w1c, w2c, hid, hp, ps, part, rsb, rst,
    pts, ptr, pcs, pga, pgs, pgr,
    gown, gcs, gcr, gxa, gya, gyb, gxb, gs2,
    ag_s, ag_r, wx_s, wx_r, wy_s, wy_r, wc_s, wc_r, pt_s, pt_r, pg_s, pg_r,
    rs_s, rs_r, gc_s, gc_r, g1_s, g1_r, g2_s, g2_r, loc,
):
    section = lax.axis_index("section")
    y = lax.axis_index("dp")
    c = lax.axis_index("expert")
    z, x = section // NX, section % NX

    def at_z(j):
        return {"section": (z + j) % NZ * NX + x, "dp": y, "expert": c}

    def at_x(r):
        return {"section": z * NX + (x + r) % NX, "dp": y, "expert": c}

    def at_y(r):
        return {"section": section, "dp": (y + r) % NY, "expert": c}

    other_core = {"section": section, "dp": y, "expert": 1 - c}

    started = []

    def send(src, dst, s_sem, r_sem, device):
        copy = pltpu.make_async_remote_copy(
            src_ref=src, dst_ref=dst, send_sem=s_sem, recv_sem=r_sem,
            device_id=device, device_id_type=MESH,
        )
        copy.start()
        started.append(copy)

    def arrived(dst, s_sem, r_sem):
        pltpu.make_async_remote_copy(
            src_ref=dst, dst_ref=dst, send_sem=s_sem, recv_sem=r_sem,
            device_id=other_core, device_id_type=MESH,
        ).wait_recv()

    x_cols = pl.ds(pl.multiple_of(x * FF, FF), FF)
    local = [
        pltpu.make_async_copy(tok_in, tu.at[0, pl.ds(0, TOK)], loc.at[0]),
        pltpu.make_async_copy(up_in, tu.at[1, pl.ds(0, TOK)], loc.at[1]),
        pltpu.make_async_copy(w1_in.at[0], w1c.at[:, x_cols], loc.at[2]),
        pltpu.make_async_copy(w2_in.at[0], w2c.at[x_cols, :], loc.at[3]),
    ]
    for copy in local:
        copy.start()

    barrier = pltpu.get_barrier_semaphore()
    peers = [at_z(j) for j in range(1, NZ)] + [at_x(r) for r in range(1, NX)]
    peers += [at_y(r) for r in range(1, NY)] + [other_core]
    for peer in peers:
        pl.semaphore_signal(barrier, inc=1, device_id=peer, device_id_type=MESH)
    pl.semaphore_wait(barrier, len(peers))

    CH = TOK // 2
    sign = (1, -1)

    def ag_valid(h, d, a):
        return h <= 3 or (h == 4 and a == d)

    def ag_place(w, h, d, a):
        return tu.at[w, pl.ds(slot_of(-sign[d] * h) * TOK + a * CH, CH)]

    def ag_send(w, h, d, a):
        if h == 1:
            src = (tok_in, up_in)[w].at[pl.ds(a * CH, CH)]
        else:
            src = ag_place(w, h - 1, d, a)
        send(src, ag_place(w, h, d, a), ag_s.at[w, d, h - 1, a], ag_r.at[w, d, h - 1, a],
             at_z(sign[d]))

    def ag_hop(w, h):
        for a in range(2):
            for d in range(2):
                if ag_valid(h, d, a):
                    arrived(ag_place(w, h, d, a), ag_s.at[w, d, h - 1, a], ag_r.at[w, d, h - 1, a])
                    if h < 4 and ag_valid(h + 1, d, a):
                        ag_send(w, h + 1, d, a)

    q_mine = (y % 2) * 2 + c
    q_next = ((y + 1) % 2) * 2 + c
    q_core = (y % 2) * 2 + 1 - c
    q_both = ((y + 1) % 2) * 2 + 1 - c

    def w_place(w, e, q, part_of=None):
        rows = D // 4 if w == 0 else FF // 4
        base, size = q * rows, rows
        if part_of is not None:
            size = rows // 2
            base = base + part_of * size
        if w == 0:
            return w1c.at[pl.ds(pl.multiple_of(base, size), size),
                          pl.ds(pl.multiple_of(e * FF, FF), FF)]
        return w2c.at[pl.ds(pl.multiple_of(e * FF + base, size), size), :]

    def wx_send(w, r):
        rows = D // 4 if w == 0 else FF // 4
        src = (w1_in, w2_in)[w].at[0, pl.ds(pl.multiple_of(q_mine * rows, rows), rows), :]
        send(src, w_place(w, x, q_mine), wx_s.at[w, r - 1], wx_r.at[w, 3 - r], at_x(r))

    def wx_relay(w, r):
        e = (x + r) % NX
        arrived(w_place(w, e, q_mine), wx_s.at[w, r - 1], wx_r.at[w, r - 1])
        for k, step in ((0, 1), (1, -1)):
            send(w_place(w, e, q_mine, k), w_place(w, e, q_mine, k),
                 wy_s.at[w, r - 1, k], wy_r.at[w, r - 1, k], at_y(step))
        send(w_place(w, e, q_mine), w_place(w, e, q_mine),
             wc_s.at[w, r - 1, 0], wc_r.at[w, r - 1, 0], other_core)

    def wy_relay(w, r):
        e = (x + r) % NX
        for k in range(2):
            arrived(w_place(w, e, q_next, k), wy_s.at[w, r - 1, k], wy_r.at[w, r - 1, k])
        send(w_place(w, e, q_next), w_place(w, e, q_next),
             wc_s.at[w, r - 1, 1], wc_r.at[w, r - 1, 1], other_core)

    def w_arrive(w, r):
        e = (x + r) % NX
        arrived(w_place(w, e, q_core), wc_s.at[w, r - 1, 0], wc_r.at[w, r - 1, 0])
        arrived(w_place(w, e, q_both), wc_s.at[w, r - 1, 1], wc_r.at[w, r - 1, 1])

    for w in range(2):
        for a in range(2):
            for d in range(2):
                ag_send(w, 1, d, a)
        for r in (1, 3, 2):
            wx_send(w, r)

    lane = lax.broadcasted_iota(jnp.int32, (TOK, TOK), 1)
    table = jnp.zeros((TOK, TOK), F32)
    for k in range(TOPK):
        e = ids[:, k:k + 1]
        table += jnp.where(lane == (e >> 2) * 8 + (e & 3), probs[:, k:k + 1], 0.0)
    pts[...] = table.T[:NZ * 8]
    for j in range(1, NZ):
        there = slot_of(-j)
        send(pts.at[pl.ds(pl.multiple_of((z + j) % NZ * 8, 8), 8)], ptr.at[pl.ds(there * 8, 8)],
             pt_s.at[j - 1], pt_r.at[there - 1], at_z(j))
    ptr[0:8, :] = pts[pl.ds(pl.multiple_of(z * 8, 8), 8), :]
    pga[...] = jnp.zeros_like(pga)

    def columns(i):
        return pl.ds(pl.multiple_of(i * FF, FF), FF)

    def block_rows(b):
        return pl.ds(b * BLOCK, BLOCK)

    def pre_block(b):
        def one(i, carry):
            pre = lax.dot_general(tu[0, block_rows(b), :], w1c[:, columns(i)], NN,
                                  preferred_element_type=F32)
            p = jnp.concatenate(
                [jnp.sum(jnp.where(lane == (2 * b + k) * 8 + i, pcs[...], 0.0), axis=1,
                         keepdims=True) for k in range(2)], axis=0)
            sig = 1.0 / (1.0 + jnp.exp(-pre))
            act = pre * sig
            hid[block_rows(b), columns(i)] = act.astype(BF16)
            hp[block_rows(b), columns(i)] = (p * act).astype(BF16)
            ps[block_rows(b), columns(i)] = p * (sig * (1.0 + pre * (1.0 - sig)))
            return carry
        lax.fori_loop(0, NX, one, 0)

    def mixed_block(b):
        def one(n, carry):
            part[0, n, block_rows(b), :] = lax.dot_general(
                hp[block_rows(b), :], w2c[:, pl.ds(pl.multiple_of(n * HALF, HALF), HALF)], NN,
                preferred_element_type=F32)
            return carry
        lax.fori_loop(0, 2, one, 0)

    def back_block(b):
        def one(i, carry):
            dhu = lax.dot_general(tu[1, block_rows(b), :], w2c[columns(i), :], NT,
                                  preferred_element_type=F32)
            col = jnp.sum(hid[block_rows(b), columns(i)].astype(F32) * dhu, axis=1, keepdims=True)
            total = pga[...]
            for k in range(2):
                total += jnp.where(lane == (2 * b + k) * 8 + i, col[k * TOK:(k + 1) * TOK], 0.0)
            pga[...] = total
            hid[block_rows(b), columns(i)] = (dhu * ps[block_rows(b), columns(i)]).astype(BF16)
            return carry
        lax.fori_loop(0, NX, one, 0)

    def input_block(b):
        def one(n, carry):
            part[1, n, block_rows(b), :] = lax.dot_general(
                hid[block_rows(b), :], w1c[pl.ds(pl.multiple_of(n * HALF, HALF), HALF), :], NT,
                preferred_element_type=F32)
            return carry
        lax.fori_loop(0, 2, one, 0)

    def weight_grad(hf):
        def one(i, carry):
            g = lax.dot_general(hp[:, columns(i)], tu[1, :, hf * HALF:(hf + 1) * HALF], TN,
                                preferred_element_type=F32).reshape(NY, 2, FF // 8, HALF)
            mine = c == 0
            gown[hf, i] = jnp.where(mine, g[:, 0], g[:, 1])
            gcs[hf, i] = jnp.where(mine, g[:, 1], g[:, 0]).astype(BF16)
            return carry
        lax.fori_loop(0, NX, one, 0)
        send(gcs.at[hf], gcr.at[hf], gc_s.at[hf], gc_r.at[hf], other_core)

    def rs_rows(d, j):
        return pl.ds(slot_of(sign[d] * j) * TOK, TOK)

    def rs_send(w, d, j, n, src):
        send(src, rsb.at[w, d, j - 1, n], rs_s.at[w, d, j - 1, n], rs_r.at[w, d, j - 1, n],
             at_z(sign[d]))

    def rs_arrived(w, d, j, n):
        arrived(rsb.at[w, d, j, n], rs_s.at[w, d, j, n], rs_r.at[w, d, j, n])

    def rs_step(w, j):
        for d in range(2):
            if j == 4:
                rst[w, d] = part[w, d, rs_rows(d, j), :].astype(BF16)
                rs_send(w, d, j, d, rst.at[w, d])
        if j == 4:
            return
        for n in (1, 0) if j == 3 else (0, 1):
            for d in range(2):
                value = part[w, n, rs_rows(d, j), :]
                if j < 3 or n == d:
                    rs_arrived(w, d, j, n)
                    value = value + rsb[w, d, j, n].astype(F32)
                rsb[w, d, j, n] = value.astype(BF16)
                rs_send(w, d, j, n, rsb.at[w, d, j, n])

    def rs_end(w, out):
        for n in range(2):
            value = part[w, n, pl.ds(0, TOK), :]
            for d in range(2):
                rs_arrived(w, d, 0, n)
                value = value + rsb[w, d, 0, n].astype(F32)
            out[:, n * HALF:(n + 1) * HALF] = value.astype(BF16)

    def grad_first(hf):
        arrived(gcr.at[hf], gc_s.at[hf], gc_r.at[hf])

        def one(i, carry):
            gcr[hf, i] = (gown[hf, i] + gcr[hf, i].astype(F32)).astype(BF16)
            return carry
        lax.fori_loop(0, NX, one, 0)
        for r in (1, 3, 2):
            if hf == 0:
                send(gcr.at[0, (x + r) % NX], gxa.at[3 - r],
                     g1_s.at[0, r - 1], g1_r.at[0, 3 - r], at_x(r))
            else:
                send(gcr.at[1, :, (y + r) % NY], gyb.at[3 - r],
                     g1_s.at[1, r - 1], g1_r.at[1, 3 - r], at_y(r))

    def grad_second(hf):
        total = gcr[0, x].astype(F32) if hf == 0 else gcr[1, :, y].astype(F32)
        landed = gxa if hf == 0 else gyb
        for k in range(3):
            arrived(landed.at[k], g1_s.at[hf, k], g1_r.at[hf, k])
            total = total + landed[k].astype(F32)
        gs2[hf] = total.astype(BF16)
        for r in (1, 3, 2):
            if hf == 0:
                send(gs2.at[0, (y + r) % NY], gya.at[3 - r],
                     g2_s.at[0, r - 1], g2_r.at[0, 3 - r], at_y(r))
            else:
                send(gs2.at[1, (x + r) % NX], gxb.at[3 - r],
                     g2_s.at[1, r - 1], g2_r.at[1, 3 - r], at_x(r))

    def grad_end(hf):
        total = gs2[0, y].astype(F32) if hf == 0 else gs2[1, x].astype(F32)
        landed = gya if hf == 0 else gxb
        for k in range(3):
            arrived(landed.at[k], g2_s.at[hf, k], g2_r.at[hf, k])
            total = total + landed[k].astype(F32)
        sgrad[0, :, hf * HALF:(hf + 1) * HALF] = total.astype(BF16)

    ag_hop(0, 1)
    for r in (1, 3, 2):
        wx_relay(0, r)
    ag_hop(0, 2)
    for r in (1, 3, 2):
        wy_relay(0, r)
    for s in range(1, NZ):
        arrived(ptr.at[pl.ds(s * 8, 8)], pt_s.at[s - 1], pt_r.at[s - 1])
    pcs[...] = jnp.concatenate([ptr[...], jnp.zeros((TOK - NZ * 8, TOK), F32)], axis=0).T
    for copy in local:
        copy.wait()
    ag_hop(0, 3)
    for r in (1, 3, 2):
        w_arrive(0, r)
    pre_block(0)
    ag_hop(0, 4)
    for r in (1, 3, 2):
        wx_relay(1, r)
    pre_block(1)
    ag_hop(1, 1)
    for r in (1, 3, 2):
        wy_relay(1, r)
    pre_block(2)
    pre_block(3)
    ag_hop(1, 2)
    for r in (1, 3, 2):
        w_arrive(1, r)
    mixed_block(3)
    mixed_block(2)
    ag_hop(1, 3)
    rs_step(0, 4)
    mixed_block(1)
    mixed_block(0)
    ag_hop(1, 4)
    rs_step(0, 3)
    weight_grad(0)
    weight_grad(1)
    rs_step(0, 2)
    grad_first(0)
    grad_first(1)
    back_block(3)
    rs_step(0, 1)
    back_block(2)
    back_block(1)
    back_block(0)
    input_block(3)
    rs_step(1, 4)
    input_block(2)
    rs_step(1, 3)
    input_block(1)
    input_block(0)

    pgs[...] = pga[...].T[:NZ * 8]
    for j in range(1, NZ):
        send(pgs.at[pl.ds(slot_of(j) * 8, 8)], pgr.at[pl.ds(pl.multiple_of(z * 8, 8), 8)],
             pg_s.at[j - 1], pg_r.at[NZ - 1 - j], at_z(j))
    pgr[pl.ds(pl.multiple_of(z * 8, 8), 8), :] = pgs[0:8, :]

    grad_second(0)
    grad_second(1)
    rs_end(0, mixed)
    rs_step(1, 2)
    rs_step(1, 1)
    grad_end(0)
    grad_end(1)

    for j in range(1, NZ):
        arrived(pgr.at[pl.ds(pl.multiple_of((z + j) % NZ * 8, 8), 8)], pg_s.at[j - 1], pg_r.at[j - 1])
    table = jnp.concatenate([pgr[...], jnp.zeros((TOK - NZ * 8, TOK), F32)], axis=0).T
    out = jnp.zeros((TOK, TOPK), F32)
    place = lax.broadcasted_iota(jnp.int32, (TOK, TOPK), 1)
    for k in range(TOPK):
        e = ids[:, k:k + 1]
        col = jnp.sum(jnp.where(lane == (e >> 2) * 8 + (e & 3), table, 0.0), axis=1, keepdims=True)
        out += jnp.where(place == k, col, 0.0)
    pgrad[...] = out

    rs_end(1, igrad)
    for copy in started:
        copy.wait_send()


def body(tokens, expert_ids, probs, first_weight, second_weight, upstream):
    any_spec = pl.BlockSpec(memory_space=pl.ANY)
    vmem_spec = pl.BlockSpec(memory_space=pltpu.VMEM)
    dma = pltpu.SemaphoreType.DMA
    scratch = [
        pltpu.VMEM((2, ROWS, D), BF16),
        pltpu.VMEM((D, NX * FF), BF16),
        pltpu.VMEM((NX * FF, D), BF16),
        pltpu.VMEM((ROWS, NX * FF), BF16),
        pltpu.VMEM((ROWS, NX * FF), BF16),
        pltpu.VMEM((ROWS, NX * FF), F32),
        pltpu.VMEM((2, 2, ROWS, HALF), F32),
        pltpu.VMEM((2, 2, 4, 2, TOK, HALF), BF16),
        pltpu.VMEM((2, 2, TOK, HALF), BF16),
        pltpu.VMEM((NZ * 8, TOK), F32),
        pltpu.VMEM((NZ * 8, TOK), F32),
        pltpu.VMEM((TOK, TOK), F32),
        pltpu.VMEM((TOK, TOK), F32),
        pltpu.VMEM((NZ * 8, TOK), F32),
        pltpu.VMEM((NZ * 8, TOK), F32),
        pltpu.VMEM((2, NX, NY, FF // 8, HALF), F32),
        pltpu.VMEM((2, NX, NY, FF // 8, HALF), BF16),
        pltpu.VMEM((2, NX, NY, FF // 8, HALF), BF16),
        pltpu.VMEM((3, NY, FF // 8, HALF), BF16),
        pltpu.VMEM((3, FF // 8, HALF), BF16),
        pltpu.VMEM((3, NX, FF // 8, HALF), BF16),
        pltpu.VMEM((3, FF // 8, HALF), BF16),
        pltpu.VMEM((2, 4, FF // 8, HALF), BF16),
        dma((2, 2, 4, 2)), dma((2, 2, 4, 2)),
        dma((2, 3)), dma((2, 3)),
        dma((2, 3, 2)), dma((2, 3, 2)),
        dma((2, 3, 2)), dma((2, 3, 2)),
        dma((NZ - 1,)), dma((NZ - 1,)),
        dma((NZ - 1,)), dma((NZ - 1,)),
        dma((2, 2, 4, 2)), dma((2, 2, 4, 2)),
        dma((2,)), dma((2,)),
        dma((2, 3)), dma((2, 3)),
        dma((2, 3)), dma((2, 3)),
        dma((4,)),
    ]
    return pl.pallas_call(
        kernel,
        out_shape=(
            jax.ShapeDtypeStruct((TOK, D), BF16),
            jax.ShapeDtypeStruct((TOK, D), BF16),
            jax.ShapeDtypeStruct((1, FF // 8, D), BF16),
            jax.ShapeDtypeStruct((TOK, TOPK), F32),
        ),
        in_specs=[any_spec] * 4 + [vmem_spec] * 2,
        out_specs=(vmem_spec,) * 4,
        scratch_shapes=scratch,
        compiler_params=pltpu.CompilerParams(
            collective_id=0, has_side_effects=True, vmem_limit_bytes=60 * 1024 * 1024
        ),
        cost_estimate=pl.CostEstimate(
            flops=2 * 5 * ROWS * D * NX * FF, bytes_accessed=8 * 1024 * 1024,
            transcendentals=ROWS * NX * FF,
        ),
    )(tokens, upstream, first_weight, second_weight, expert_ids, probs)


def solution(mesh):
    everything = P(("section", "dp", "expert"), None)
    return jax.shard_map(
        body,
        mesh=mesh,
        in_specs=(everything, everything, everything, P("section", None, None),
                  P("section", None, None), everything),
        out_specs=(everything, everything, P("section", ("dp", "expert"), None), everything),
        check_vma=False,
    )
```

time: 478 us -> 126 us (0.26); the launches traced: 469 us -> 126 us
  blocking collectives: 171 us -> 0 us
  Pallas kernels: 0 us -> 119 us
  local copies, waits for them, and re-layouts: 103 us -> 7.02 us
  waiting for transfers between devices: 84.4 us -> 0 us
  other arithmetic: 56 us -> 0 us
  starting transfers between devices: 33.9 us -> 0 us
  matrix products: 17.7 us -> 0 us
    unnamed x1 -> x0, blocking collectives: 171 us -> none
    pallas_call x0 -> x1, Pallas kernels: none -> 119 us  [body(): pl.pallas_call(kernel, out_shape=(jax.ShapeDtypeStruct((TOK, D), BF16), j...]
    all_to_all x4 -> x0, waiting for transfers between devices: 84.4 us -> none  [the longest x1 52.3 us: body(): lax.all_to_all(token_slots, 'section', split_axis=0, concat_axis=2, tiled...]
    unnamed x30 -> x11, local copies, waits for them, and re-layouts: 51.2 us -> 5.52 us
    unnamed x2 -> x0, other arithmetic: 34 us -> none
    all_to_all x4 -> x0, starting transfers between devices: 33.9 us -> none  [the longest x1 11.8 us: body(): lax.all_to_all(token_slots, 'section', split_axis=0, concat_axis=2, tiled...]
    reshape x2 -> x0, local copies, waits for them, and re-layouts: 24.2 us -> none  [the longest x1 18.2 us: body(): expert_out.reshape(1, local_experts, sections * SLOT_CAPACITY, row_width)]
    dot_general x4 -> x0, matrix products: 17.7 us -> none  [the longest x1 7.34 us: body(): jnp.einsum('erf,edf->erd', pre_grad, first_weight, preferred_element_type...]
  transfers between devices with their start and end apart: 4 -> 0, of which waited for: 3 -> 0; matrix products, arithmetic and copies ran while one was open for 28% -> 0% of each run, Pallas kernels for 0% -> 0%
where the time goes in v1:
time: 126 us
  Pallas kernels  119 us (94%)
  local copies, waits for them, and re-layouts  7.02 us (6%)
    pallas_call x1, Pallas kernels, body(): pl.pallas_call(kernel, out_shape=(jax.ShapeDtypeStruct((TOK, D), BF16), j...  119 us
    unnamed x11, local copies, waits for them, and re-layouts  5.52 us

profile of v1, /device:TPU:2, one launch (start us, length us, event | category | flops | bytes accessed | tf_op | source)
XLA Modules:
  0.0 126.3 jit_solution(12402364045607275726)
XLA Ops:
  0.6 0.0 copy-start.2
  0.6 1.4 %copy.10.ids = s32[128,8]{1,0:T(8,128)} copy(s32[128,8]{0,1:T(8,128)} %param.7) | data formatting | bytes 8192 | tf_op args[1]
  2.1 0.0 copy-done.2
  2.1 0.7 copy.11.probs
  2.8 118.6 %shard_map.93 = (bf16[128,1024]{1,0:T(8,128)(2,1)}, bf16[128,1024]{1,0:T(8,128)(2,1)}, bf16[1,64,1024]{2,1,0:T(8,128)(2,1)}, f32[128,8]{1,0:T(8,128)}) custom-call(bf16[128,1024]{1,0:T(8,128)(2,1)} %tok_in.1, bf16[128,1024]{1,0:T(8,128)(2,1)} %up_in.1, bf16[1,1024,512]{2,1,0:T(8,128)(2,1)} %w1_in.1, bf16[1,512,1024]{2,1,0:T(8,128)(2,1)} %w2_in.1, ...), custom_call_target="tpu_custom_call" | custom-call | flops 21474836480 | bytes 8388608 | tf_op jit(solution)/shard_map/pallas_call | solution.py:432
  121.4 1.5 %copy.12 = f32[128,8]{0,1:T(8,128)} copy(f32[128,8]{1,0:T(8,128)} %get-tuple-element.7) | data formatting | bytes 8192 | tf_op jit(solution)/shard_map/pallas_call | solution.py:432
  122.9 0.0 copy-start
  122.9 1.7 %copy.16 = bf16[128,1024]{1,0:T(8,128)(2,1)} copy(bf16[128,1024]{1,0:T(8,128)(2,1)} %get-tuple-element.12) | data formatting | bytes 524288
  124.6 0.0 copy-done
  124.6 0.0 copy-start.1
  124.6 0.7 copy.17
  125.3 0.3 copy-done.1
  125.6 0.7 copy.18
Async XLA Ops:
  0.6 1.4 %copy-start.2 = (f32[128,8]{0,1:T(8,128)S(1)}, f32[128,8]{0,1:T(8,128)}, u32[]{:S(2)}) copy-start(f32[128,8]{0,1:T(8,128)} %param.8) | copy-start | bytes 12292
  122.9 1.7 %copy-start = (bf16[128,1024]{1,0:T(8,128)(2,1)S(1)}, bf16[128,1024]{1,0:T(8,128)(2,1)}, u32[]{:S(2)}) copy-start(bf16[128,1024]{1,0:T(8,128)(2,1)} %get-tuple-element.13) | copy-start | bytes 786436
  124.6 1.0 copy-start.1

commit v2 on v1

--- a/solution.py
+++ b/solution.py
@@ -162,11 +162,16 @@
             wx_send(w, r)
 
     lane = lax.broadcasted_iota(jnp.int32, (TOK, TOK), 1)
-    table = jnp.zeros((TOK, TOK), F32)
+    place = lax.broadcasted_iota(jnp.int32, (NZ * 8, TOK), 0)
+
+    def place_of(k):
+        e = ids[k:k + 1, :]
+        return (e >> 2) * 8 + (e & 3)
+
+    table = jnp.zeros((NZ * 8, TOK), F32)
     for k in range(TOPK):
-        e = ids[:, k:k + 1]
-        table += jnp.where(lane == (e >> 2) * 8 + (e & 3), probs[:, k:k + 1], 0.0)
-    pts[...] = table.T[:NZ * 8]
+        table += jnp.where(place == place_of(k), probs[k:k + 1, :], 0.0)
+    pts[...] = table
     for j in range(1, NZ):
         there = slot_of(-j)
         send(pts.at[pl.ds(pl.multiple_of((z + j) % NZ * 8, 8), 8)], ptr.at[pl.ds(there * 8, 8)],
@@ -311,53 +316,55 @@
     for r in (1, 3, 2):
         wx_relay(0, r)
     ag_hop(0, 2)
-    for r in (1, 3, 2):
-        wy_relay(0, r)
     for s in range(1, NZ):
         arrived(ptr.at[pl.ds(s * 8, 8)], pt_s.at[s - 1], pt_r.at[s - 1])
     pcs[...] = jnp.concatenate([ptr[...], jnp.zeros((TOK - NZ * 8, TOK), F32)], axis=0).T
     for copy in local:
         copy.wait()
+    ag_hop(1, 1)
+    for r in (1, 3, 2):
+        wy_relay(0, r)
     ag_hop(0, 3)
     for r in (1, 3, 2):
+        wx_relay(1, r)
+    for r in (1, 3, 2):
         w_arrive(0, r)
+    ag_hop(1, 2)
     pre_block(0)
     ag_hop(0, 4)
-    for r in (1, 3, 2):
-        wx_relay(1, r)
     pre_block(1)
-    ag_hop(1, 1)
+    ag_hop(1, 3)
     for r in (1, 3, 2):
         wy_relay(1, r)
+    pre_block(3)
     pre_block(2)
-    pre_block(3)
-    ag_hop(1, 2)
     for r in (1, 3, 2):
         w_arrive(1, r)
     mixed_block(3)
+    rs_step(0, 4)
+    ag_hop(1, 4)
     mixed_block(2)
-    ag_hop(1, 3)
-    rs_step(0, 4)
+    rs_step(0, 3)
+    back_block(3)
+    input_block(3)
+    rs_step(1, 4)
     mixed_block(1)
+    rs_step(0, 2)
+    back_block(2)
+    input_block(2)
+    rs_step(1, 3)
     mixed_block(0)
-    ag_hop(1, 4)
-    rs_step(0, 3)
+    rs_step(0, 1)
     weight_grad(0)
     weight_grad(1)
-    rs_step(0, 2)
+    back_block(1)
+    input_block(1)
+    rs_step(1, 2)
     grad_first(0)
     grad_first(1)
-    back_block(3)
-    rs_step(0, 1)
-    back_block(2)
-    back_block(1)
     back_block(0)
-    input_block(3)
-    rs_step(1, 4)
-    input_block(2)
-    rs_step(1, 3)
-    input_block(1)
     input_block(0)
+    rs_step(1, 1)
 
     pgs[...] = pga[...].T[:NZ * 8]
     for j in range(1, NZ):
@@ -365,28 +372,26 @@
              pg_s.at[j - 1], pg_r.at[NZ - 1 - j], at_z(j))
     pgr[pl.ds(pl.multiple_of(z * 8, 8), 8), :] = pgs[0:8, :]
 
+    rs_end(0, mixed)
     grad_second(0)
     grad_second(1)
-    rs_end(0, mixed)
-    rs_step(1, 2)
-    rs_step(1, 1)
     grad_end(0)
     grad_end(1)
 
     for j in range(1, NZ):
         arrived(pgr.at[pl.ds(pl.multiple_of((z + j) % NZ * 8, 8), 8)], pg_s.at[j - 1], pg_r.at[j - 1])
-    table = jnp.concatenate([pgr[...], jnp.zeros((TOK - NZ * 8, TOK), F32)], axis=0).T
-    out = jnp.zeros((TOK, TOPK), F32)
-    place = lax.broadcasted_iota(jnp.int32, (TOK, TOPK), 1)
     for k in range(TOPK):
-        e = ids[:, k:k + 1]
-        col = jnp.sum(jnp.where(lane == (e >> 2) * 8 + (e & 3), table, 0.0), axis=1, keepdims=True)
-        out += jnp.where(place == k, col, 0.0)
-    pgrad[...] = out
+        pgrad[k:k + 1, :] = jnp.sum(jnp.where(place == place_of(k), pgr[...], 0.0), axis=0,
+                                    keepdims=True)
 
     rs_end(1, igrad)
     for copy in started:
         copy.wait_send()
+
+
+def hand_over(a0, a1, a2, a3, b0, b1, b2, b3):
+    for a, b in ((a0, b0), (a1, b1), (a2, b2), (a3, b3)):
+        b[...] = a[...]
 
 
 def body(tokens, expert_ids, probs, first_weight, second_weight, upstream):
@@ -429,13 +434,13 @@
         dma((2, 3)), dma((2, 3)),
         dma((4,)),
     ]
-    return pl.pallas_call(
+    results = pl.pallas_call(
         kernel,
         out_shape=(
             jax.ShapeDtypeStruct((TOK, D), BF16),
             jax.ShapeDtypeStruct((TOK, D), BF16),
             jax.ShapeDtypeStruct((1, FF // 8, D), BF16),
-            jax.ShapeDtypeStruct((TOK, TOPK), F32),
+            jax.ShapeDtypeStruct((TOPK, TOK), F32),
         ),
         in_specs=[any_spec] * 4 + [vmem_spec] * 2,
         out_specs=(vmem_spec,) * 4,
@@ -447,7 +452,14 @@
             flops=2 * 5 * ROWS * D * NX * FF, bytes_accessed=8 * 1024 * 1024,
             transcendentals=ROWS * NX * FF,
         ),
-    )(tokens, upstream, first_weight, second_weight, expert_ids, probs)
+    )(tokens, upstream, first_weight, second_weight, expert_ids.T, probs.T)
+    mixed, igrad, sgrad, pgrad = pl.pallas_call(
+        hand_over,
+        out_shape=tuple(jax.ShapeDtypeStruct(r.shape, r.dtype) for r in results),
+        in_specs=[vmem_spec] * 4,
+        out_specs=(vmem_spec,) * 4,
+    )(*results)
+    return mixed, igrad, sgrad, pgrad.T
 
 
 def solution(mesh):

time: 126 us -> 115 us (0.913); the launches traced: 126 us -> 113 us
  local copies, waits for them, and re-layouts: 7.02 us -> 0 us
  Pallas kernels: 119 us -> 112 us
    pallas_call x1, Pallas kernels: 119 us -> 111 us  [body(): pl.pallas_call(kernel, out_shape=(jax.ShapeDtypeStruct((TOK, D), BF16), j...]
    unnamed x11 -> x0, local copies, waits for them, and re-layouts: 5.52 us -> none
    pallas_call x0 -> x1, Pallas kernels: none -> 1.91 us  [body(): pl.pallas_call(hand_over, out_shape=tuple((jax.ShapeDtypeStruct(r.shape,...]
    pallas_call x1 -> x0, local copies, waits for them, and re-layouts: 1.5 us -> none  [body(): pl.pallas_call(kernel, out_shape=(jax.ShapeDtypeStruct((TOK, D), BF16), j...]
where the time goes in v2:
time: 115 us; the launch traced here: 113 us
  Pallas kernels  112 us (97%)
    pallas_call x1, Pallas kernels, body(): pl.pallas_call(kernel, out_shape=(jax.ShapeDtypeStruct((TOK, D), BF16), j...  111 us

profile of v2, /device:TPU:2, one launch (start us, length us, event | category | flops | bytes accessed | tf_op | source)
XLA Modules:
  0.0 113.1 jit_solution(8474883816045647975)
XLA Ops:
  0.6 110.6 %shard_map.93 = (bf16[128,1024]{1,0:T(8,128)(2,1)}, bf16[128,1024]{1,0:T(8,128)(2,1)}, bf16[1,64,1024]{2,1,0:T(8,128)(2,1)}, f32[8,128]{1,0:T(8,128)}) custom-call(bf16[128,1024]{1,0:T(8,128)(2,1)} %tok_in.1, bf16[128,1024]{1,0:T(8,128)(2,1)} %up_in.1, bf16[1,1024,512]{2,1,0:T(8,128)(2,1)} %w1_in.1, bf16[1,512,1024]{2,1,0:T(8,128)(2,1)} %w2_in.1, ...), custom_call_target="tpu_custom_call" | custom-call | flops 21474836480 | bytes 8388608 | tf_op jit(solution)/shard_map/pallas_call | solution.py:437
  111.2 1.9 %shard_map.94 = (bf16[128,1024]{1,0:T(8,128)(2,1)}, bf16[128,1024]{1,0:T(8,128)(2,1)}, bf16[1,64,1024]{2,1,0:T(8,128)(2,1)}, f32[8,128]{1,0:T(8,128)}) custom-call(bf16[128,1024]{1,0:T(8,128)(2,1)} %get-tuple-element.12.a0, bf16[128,1024]{1,0:T(8,128)(2,1)} %get-tuple-element.13.a1, bf16[1,64,1024]{2,1,0:T(8,128)(2,1)} %get-tuple-element.14.a2, ...), custom_call_target="tpu_custom_call" | custom-call | tf_op jit(solution)/shard_map/pallas_call | solution.py:456

commit v3 on v2

--- a/solution.py
+++ b/solution.py
@@ -104,8 +104,8 @@
         send(src, ag_place(w, h, d, a), ag_s.at[w, d, h - 1, a], ag_r.at[w, d, h - 1, a],
              at_z(sign[d]))
 
-    def ag_hop(w, h):
-        for a in range(2):
+    def ag_hop(w, h, *chunks):
+        for a in chunks or (0, 1):
             for d in range(2):
                 if ag_valid(h, d, a):
                     arrived(ag_place(w, h, d, a), ag_s.at[w, d, h - 1, a], ag_r.at[w, d, h - 1, a])
@@ -182,50 +182,53 @@
     def columns(i):
         return pl.ds(pl.multiple_of(i * FF, FF), FF)
 
-    def block_rows(b):
-        return pl.ds(b * BLOCK, BLOCK)
-
-    def pre_block(b):
+    def pre_block(first, size, e_from=0, e_to=NX):
+        rows = pl.ds(first * TOK, size * TOK)
+
         def one(i, carry):
-            pre = lax.dot_general(tu[0, block_rows(b), :], w1c[:, columns(i)], NN,
+            pre = lax.dot_general(tu[0, rows, :], w1c[:, columns(i)], NN,
                                   preferred_element_type=F32)
             p = jnp.concatenate(
-                [jnp.sum(jnp.where(lane == (2 * b + k) * 8 + i, pcs[...], 0.0), axis=1,
-                         keepdims=True) for k in range(2)], axis=0)
-            sig = 1.0 / (1.0 + jnp.exp(-pre))
+                [jnp.sum(jnp.where(lane == (first + k) * 8 + i, pcs[...], 0.0), axis=1,
+                         keepdims=True) for k in range(size)], axis=0)
+            sig = 0.5 * jnp.tanh(0.5 * pre) + 0.5
             act = pre * sig
-            hid[block_rows(b), columns(i)] = act.astype(BF16)
-            hp[block_rows(b), columns(i)] = (p * act).astype(BF16)
-            ps[block_rows(b), columns(i)] = p * (sig * (1.0 + pre * (1.0 - sig)))
-            return carry
-        lax.fori_loop(0, NX, one, 0)
-
-    def mixed_block(b):
+            hid[rows, columns(i)] = act.astype(BF16)
+            hp[rows, columns(i)] = (p * act).astype(BF16)
+            ps[rows, columns(i)] = p * (sig * (1.0 + pre * (1.0 - sig)))
+            return carry
+        lax.fori_loop(e_from, e_to, one, 0)
+
+    def mixed_block(first, size):
+        rows = pl.ds(first * TOK, size * TOK)
+
         def one(n, carry):
-            part[0, n, block_rows(b), :] = lax.dot_general(
-                hp[block_rows(b), :], w2c[:, pl.ds(pl.multiple_of(n * HALF, HALF), HALF)], NN,
-                preferred_element_type=F32)
+            part[0, n, rows, :] = lax.dot_general(hp[rows, :], w2c[:, columns(n)], NN,
+                                                  preferred_element_type=F32)
             return carry
         lax.fori_loop(0, 2, one, 0)
 
-    def back_block(b):
+    def back_block(first, size, e_from=0, e_to=NX):
+        rows = pl.ds(first * TOK, size * TOK)
+
         def one(i, carry):
-            dhu = lax.dot_general(tu[1, block_rows(b), :], w2c[columns(i), :], NT,
+            dhu = lax.dot_general(tu[1, rows, :], w2c[columns(i), :], NT,
                                   preferred_element_type=F32)
-            col = jnp.sum(hid[block_rows(b), columns(i)].astype(F32) * dhu, axis=1, keepdims=True)
+            col = jnp.sum(hid[rows, columns(i)].astype(F32) * dhu, axis=1, keepdims=True)
             total = pga[...]
-            for k in range(2):
-                total += jnp.where(lane == (2 * b + k) * 8 + i, col[k * TOK:(k + 1) * TOK], 0.0)
+            for k in range(size):
+                total += jnp.where(lane == (first + k) * 8 + i, col[k * TOK:(k + 1) * TOK], 0.0)
             pga[...] = total
-            hid[block_rows(b), columns(i)] = (dhu * ps[block_rows(b), columns(i)]).astype(BF16)
-            return carry
-        lax.fori_loop(0, NX, one, 0)
-
-    def input_block(b):
+            hid[rows, columns(i)] = (dhu * ps[rows, columns(i)]).astype(BF16)
+            return carry
+        lax.fori_loop(e_from, e_to, one, 0)
+
+    def input_block(first, size):
+        rows = pl.ds(first * TOK, size * TOK)
+
         def one(n, carry):
-            part[1, n, block_rows(b), :] = lax.dot_general(
-                hid[block_rows(b), :], w1c[pl.ds(pl.multiple_of(n * HALF, HALF), HALF), :], NT,
-                preferred_element_type=F32)
+            part[1, n, rows, :] = lax.dot_general(hid[rows, :], w1c[columns(n), :], NT,
+                                                  preferred_element_type=F32)
             return carry
         lax.fori_loop(0, 2, one, 0)
 
@@ -250,21 +253,24 @@
     def rs_arrived(w, d, j, n):
         arrived(rsb.at[w, d, j, n], rs_s.at[w, d, j, n], rs_r.at[w, d, j, n])
 
+    def rs_start(w):
+        for d in range(2):
+            rst[w, d] = part[w, d, rs_rows(d, 4), :].astype(BF16)
+            rs_send(w, d, 4, d, rst.at[w, d])
+        for d in range(2):
+            rsb[w, d, 3, 1 - d] = part[w, 1 - d, rs_rows(d, 3), :].astype(BF16)
+            rs_send(w, d, 3, 1 - d, rsb.at[w, d, 3, 1 - d])
+
     def rs_step(w, j):
-        for d in range(2):
-            if j == 4:
-                rst[w, d] = part[w, d, rs_rows(d, j), :].astype(BF16)
-                rs_send(w, d, j, d, rst.at[w, d])
-        if j == 4:
-            return
-        for n in (1, 0) if j == 3 else (0, 1):
+        for n in range(2):
             for d in range(2):
-                value = part[w, n, rs_rows(d, j), :]
-                if j < 3 or n == d:
-                    rs_arrived(w, d, j, n)
-                    value = value + rsb[w, d, j, n].astype(F32)
-                rsb[w, d, j, n] = value.astype(BF16)
-                rs_send(w, d, j, n, rsb.at[w, d, j, n])
+                half = 1 - d if n == 0 else d
+                if j == 3 and n == 0:
+                    continue
+                rs_arrived(w, d, j, half)
+                value = part[w, half, rs_rows(d, j), :] + rsb[w, d, j, half].astype(F32)
+                rsb[w, d, j, half] = value.astype(BF16)
+                rs_send(w, d, j, half, rsb.at[w, d, j, half])
 
     def rs_end(w, out):
         for n in range(2):
@@ -312,78 +318,86 @@
             total = total + landed[k].astype(F32)
         sgrad[0, :, hf * HALF:(hf + 1) * HALF] = total.astype(BF16)
 
+    def p_columns():
+        for k in range(1, NZ):
+            arrived(ptr.at[pl.ds(k * 8, 8)], pt_s.at[k - 1], pt_r.at[k - 1])
+        pcs[...] = jnp.concatenate([ptr[...], jnp.zeros((TOK - NZ * 8, TOK), F32)], axis=0).T
+
+    def p_back():
+        pgs[...] = pga[...].T[:NZ * 8]
+        for j in range(1, NZ):
+            send(pgs.at[pl.ds(slot_of(j) * 8, 8)], pgr.at[pl.ds(pl.multiple_of(z * 8, 8), 8)],
+                 pg_s.at[j - 1], pg_r.at[NZ - 1 - j], at_z(j))
+        pgr[pl.ds(pl.multiple_of(z * 8, 8), 8), :] = pgs[0:8, :]
+
+    def p_end():
+        for j in range(1, NZ):
+            arrived(pgr.at[pl.ds(pl.multiple_of((z + j) % NZ * 8, 8), 8)],
+                    pg_s.at[j - 1], pg_r.at[j - 1])
+        for k in range(TOPK):
+            pgrad[k:k + 1, :] = jnp.sum(jnp.where(place == place_of(k), pgr[...], 0.0), axis=0,
+                                        keepdims=True)
+
+    def each(f, w):
+        for r in (1, 3, 2):
+            f(w, r)
+
     ag_hop(0, 1)
-    for r in (1, 3, 2):
-        wx_relay(0, r)
-    ag_hop(0, 2)
-    for s in range(1, NZ):
-        arrived(ptr.at[pl.ds(s * 8, 8)], pt_s.at[s - 1], pt_r.at[s - 1])
-    pcs[...] = jnp.concatenate([ptr[...], jnp.zeros((TOK - NZ * 8, TOK), F32)], axis=0).T
+    each(wx_relay, 0)
+    ag_hop(1, 1, 0)
+    p_columns()
     for copy in local:
         copy.wait()
-    ag_hop(1, 1)
-    for r in (1, 3, 2):
-        wy_relay(0, r)
-    ag_hop(0, 3)
-    for r in (1, 3, 2):
-        wx_relay(1, r)
-    for r in (1, 3, 2):
-        w_arrive(0, r)
-    ag_hop(1, 2)
-    pre_block(0)
+    ag_hop(1, 1, 1)
+    each(wy_relay, 0)
+    ag_hop(0, 2, 0)
+    each(wx_relay, 1)
+    ag_hop(0, 2, 1)
+    each(w_arrive, 0)
+    pre_block(0, 4, 0, 2)
+    ag_hop(1, 2, 0)
+    pre_block(0, 4, 2, 4)
+    ag_hop(1, 2, 1)
+    each(wy_relay, 1)
+    ag_hop(0, 3, 0)
+    ag_hop(0, 3, 1)
+    each(w_arrive, 1)
+    pre_block(4, 2)
+    back_block(0, 4, 0, 1)
+    ag_hop(1, 3, 0)
+    back_block(0, 4, 1, 3)
+    ag_hop(1, 3, 1)
+    back_block(4, 2)
+    mixed_block(4, 2)
     ag_hop(0, 4)
-    pre_block(1)
-    ag_hop(1, 3)
-    for r in (1, 3, 2):
-        wy_relay(1, r)
-    pre_block(3)
-    pre_block(2)
-    for r in (1, 3, 2):
-        w_arrive(1, r)
-    mixed_block(3)
-    rs_step(0, 4)
+    pre_block(6, 2)
+    mixed_block(6, 2)
+    rs_start(0)
+    input_block(4, 2)
     ag_hop(1, 4)
-    mixed_block(2)
+    back_block(6, 2)
+    input_block(6, 2)
+    rs_start(1)
     rs_step(0, 3)
-    back_block(3)
-    input_block(3)
-    rs_step(1, 4)
-    mixed_block(1)
+    weight_grad(0)
+    grad_first(0)
+    mixed_block(0, 4)
     rs_step(0, 2)
-    back_block(2)
-    input_block(2)
+    back_block(0, 4, 3, 4)
     rs_step(1, 3)
-    mixed_block(0)
+    weight_grad(1)
+    input_block(0, 4)
     rs_step(0, 1)
-    weight_grad(0)
-    weight_grad(1)
-    back_block(1)
-    input_block(1)
+    grad_first(1)
     rs_step(1, 2)
-    grad_first(0)
-    grad_first(1)
-    back_block(0)
-    input_block(0)
+    p_back()
+    grad_second(0)
     rs_step(1, 1)
-
-    pgs[...] = pga[...].T[:NZ * 8]
-    for j in range(1, NZ):
-        send(pgs.at[pl.ds(slot_of(j) * 8, 8)], pgr.at[pl.ds(pl.multiple_of(z * 8, 8), 8)],
-             pg_s.at[j - 1], pg_r.at[NZ - 1 - j], at_z(j))
-    pgr[pl.ds(pl.multiple_of(z * 8, 8), 8), :] = pgs[0:8, :]
-
+    grad_second(1)
     rs_end(0, mixed)
-    grad_second(0)
-    grad_second(1)
+    p_end()
     grad_end(0)
     grad_end(1)
-
-    for j in range(1, NZ):
-        arrived(pgr.at[pl.ds(pl.multiple_of((z + j) % NZ * 8, 8), 8)], pg_s.at[j - 1], pg_r.at[j - 1])
-    for k in range(TOPK):
-        pgrad[k:k + 1, :] = jnp.sum(jnp.where(place == place_of(k), pgr[...], 0.0), axis=0,
-                                    keepdims=True)
-
     rs_end(1, igrad)
     for copy in started:
         copy.wait_send()

time: 115 us -> 104 us (0.904); the launches traced: 113 us -> 103 us
  Pallas kernels: 112 us -> 103 us
    pallas_call x1, Pallas kernels: 111 us -> 101 us  [body(): pl.pallas_call(kernel, out_shape=(jax.ShapeDtypeStruct((TOK, D), BF16), j...]
where the time goes in v3:
time: 104 us; the launch traced here: 103 us
  Pallas kernels  103 us (99%)
    pallas_call x1, Pallas kernels, body(): pl.pallas_call(kernel, out_shape=(jax.ShapeDtypeStruct((TOK, D), BF16), j...  101 us

profile of v3, /device:TPU:2, one launch (start us, length us, event | category | flops | bytes accessed | tf_op | source)
XLA Modules:
  0.0 103.5 jit_solution(3576925253639070935)
XLA Ops:
  0.6 100.9 %shard_map.93 = (bf16[128,1024]{1,0:T(8,128)(2,1)}, bf16[128,1024]{1,0:T(8,128)(2,1)}, bf16[1,64,1024]{2,1,0:T(8,128)(2,1)}, f32[8,128]{1,0:T(8,128)}) custom-call(bf16[128,1024]{1,0:T(8,128)(2,1)} %tok_in.1, bf16[128,1024]{1,0:T(8,128)(2,1)} %up_in.1, bf16[1,1024,512]{2,1,0:T(8,128)(2,1)} %w1_in.1, bf16[1,512,1024]{2,1,0:T(8,128)(2,1)} %w2_in.1, ...), custom_call_target="tpu_custom_call" | custom-call | flops 21474836480 | bytes 8388608 | tf_op jit(solution)/shard_map/pallas_call | solution.py:451
  101.6 1.9 %shard_map.94 = (bf16[128,1024]{1,0:T(8,128)(2,1)}, bf16[128,1024]{1,0:T(8,128)(2,1)}, bf16[1,64,1024]{2,1,0:T(8,128)(2,1)}, f32[8,128]{1,0:T(8,128)}) custom-call(bf16[128,1024]{1,0:T(8,128)(2,1)} %get-tuple-element.12.a0, bf16[128,1024]{1,0:T(8,128)(2,1)} %get-tuple-element.13.a1, bf16[1,64,1024]{2,1,0:T(8,128)(2,1)} %get-tuple-element.14.a2, ...), custom_call_target="tpu_custom_call" | custom-call | tf_op jit(solution)/shard_map/pallas_call | solution.py:470

commit v4 on v3

--- a/solution.py
+++ b/solution.py
@@ -343,63 +343,68 @@
             f(w, r)
 
     ag_hop(0, 1)
-    each(wx_relay, 0)
+    wx_relay(0, 1)
+    wx_relay(0, 3)
     ag_hop(1, 1, 0)
+    wx_relay(0, 2)
+    ag_hop(1, 1, 1)
     p_columns()
     for copy in local:
         copy.wait()
-    ag_hop(1, 1, 1)
-    each(wy_relay, 0)
+    wy_relay(0, 1)
+    wy_relay(0, 3)
     ag_hop(0, 2, 0)
+    wy_relay(0, 2)
+    ag_hop(0, 2, 1)
     each(wx_relay, 1)
-    ag_hop(0, 2, 1)
+    ag_hop(1, 2, 0)
     each(w_arrive, 0)
     pre_block(0, 4, 0, 2)
-    ag_hop(1, 2, 0)
+    ag_hop(1, 2, 1)
     pre_block(0, 4, 2, 4)
-    ag_hop(1, 2, 1)
     each(wy_relay, 1)
-    ag_hop(0, 3, 0)
-    ag_hop(0, 3, 1)
+    ag_hop(0, 3)
+    pre_block(4, 3)
+    ag_hop(1, 3, 0)
     each(w_arrive, 1)
-    pre_block(4, 2)
+    mixed_block(4, 3)
+    ag_hop(1, 3, 1)
     back_block(0, 4, 0, 1)
-    ag_hop(1, 3, 0)
-    back_block(0, 4, 1, 3)
-    ag_hop(1, 3, 1)
-    back_block(4, 2)
-    mixed_block(4, 2)
     ag_hop(0, 4)
-    pre_block(6, 2)
-    mixed_block(6, 2)
+    pre_block(7, 1)
+    mixed_block(7, 1)
     rs_start(0)
-    input_block(4, 2)
+    back_block(4, 3)
     ag_hop(1, 4)
-    back_block(6, 2)
-    input_block(6, 2)
+    back_block(7, 1)
+    rs_step(0, 3)
+    input_block(4, 4)
     rs_start(1)
-    rs_step(0, 3)
     weight_grad(0)
-    grad_first(0)
     mixed_block(0, 4)
     rs_step(0, 2)
-    back_block(0, 4, 3, 4)
+    grad_first(0)
     rs_step(1, 3)
     weight_grad(1)
-    input_block(0, 4)
+    back_block(0, 4, 1, 3)
     rs_step(0, 1)
     grad_first(1)
+    back_block(0, 4, 3, 4)
+    input_block(0, 4)
     rs_step(1, 2)
+    grad_second(0)
     p_back()
-    grad_second(0)
+    early = len(started)
     rs_step(1, 1)
     grad_second(1)
     rs_end(0, mixed)
     p_end()
     grad_end(0)
     grad_end(1)
+    for copy in started[:early]:
+        copy.wait_send()
     rs_end(1, igrad)
-    for copy in started:
+    for copy in started[early:]:
         copy.wait_send()
 
 

time: 104 us -> 100 us (0.962)
  Pallas kernels: 103 us -> 98.3 us
    pallas_call x1, Pallas kernels: 101 us -> 96.4 us  [body(): pl.pallas_call(kernel, out_shape=(jax.ShapeDtypeStruct((TOK, D), BF16), j...]
where the time goes in v4:
time: 100 us; the launch traced here: 98.9 us
  Pallas kernels  98.3 us (98%)
    pallas_call x1, Pallas kernels, body(): pl.pallas_call(kernel, out_shape=(jax.ShapeDtypeStruct((TOK, D), BF16), j...  96.4 us

profile of v4, /device:TPU:2, one launch (start us, length us, event | category | flops | bytes accessed | tf_op | source)
XLA Modules:
  0.0 98.9 jit_solution(16800328984096814846)
XLA Ops:
  0.6 96.4 %shard_map.93 = (bf16[128,1024]{1,0:T(8,128)(2,1)}, bf16[128,1024]{1,0:T(8,128)(2,1)}, bf16[1,64,1024]{2,1,0:T(8,128)(2,1)}, f32[8,128]{1,0:T(8,128)}) custom-call(bf16[128,1024]{1,0:T(8,128)(2,1)} %tok_in.1, bf16[128,1024]{1,0:T(8,128)(2,1)} %up_in.1, bf16[1,1024,512]{2,1,0:T(8,128)(2,1)} %w1_in.1, bf16[1,512,1024]{2,1,0:T(8,128)(2,1)} %w2_in.1, ...), custom_call_target="tpu_custom_call" | custom-call | flops 21474836480 | bytes 8388608 | tf_op jit(solution)/shard_map/pallas_call | solution.py:456
  97.0 1.9 %shard_map.94 = (bf16[128,1024]{1,0:T(8,128)(2,1)}, bf16[128,1024]{1,0:T(8,128)(2,1)}, bf16[1,64,1024]{2,1,0:T(8,128)(2,1)}, f32[8,128]{1,0:T(8,128)}) custom-call(bf16[128,1024]{1,0:T(8,128)(2,1)} %get-tuple-element.12.a0, bf16[128,1024]{1,0:T(8,128)(2,1)} %get-tuple-element.13.a1, bf16[1,64,1024]{2,1,0:T(8,128)(2,1)} %get-tuple-element.14.a2, ...), custom_call_target="tpu_custom_call" | custom-call | tf_op jit(solution)/shard_map/pallas_call | solution.py:475

commit v5 on v4

--- a/solution.py
+++ b/solution.py
@@ -30,8 +30,9 @@
 
 
 def kernel(
-    tok_in, up_in, w1_in, w2_in, ids, probs,
-    mixed, igrad, sgrad, pgrad,
+    tok_in, up_in, w1_in, w2_in, ids_in, probs_in,
+    mixed_out, igrad_out, sgrad_out, pgrad_out,
+    ids, probs, mixed, igrad, sgrad, pgrad,
     tu, w1c, w2c, hid, hp, ps, part, rsb, rst,
     pts, ptr, pcs, pga, pgs, pgr,
     gown, gcs, gcr, gxa, gya, gyb, gxb, gs2,
@@ -77,7 +78,11 @@
         pltpu.make_async_copy(w1_in.at[0], w1c.at[:, x_cols], loc.at[2]),
         pltpu.make_async_copy(w2_in.at[0], w2c.at[x_cols, :], loc.at[3]),
     ]
-    for copy in local:
+    router = [
+        pltpu.make_async_copy(ids_in, ids, loc.at[4]),
+        pltpu.make_async_copy(probs_in, probs, loc.at[5]),
+    ]
+    for copy in router + local:
         copy.start()
 
     barrier = pltpu.get_barrier_semaphore()
@@ -163,6 +168,9 @@
 
     lane = lax.broadcasted_iota(jnp.int32, (TOK, TOK), 1)
     place = lax.broadcasted_iota(jnp.int32, (NZ * 8, TOK), 0)
+
+    for copy in router:
+        copy.wait()
 
     def place_of(k):
         e = ids[k:k + 1, :]
@@ -399,11 +407,23 @@
     grad_second(1)
     rs_end(0, mixed)
     p_end()
+    results = [
+        pltpu.make_async_copy(mixed, mixed_out, loc.at[6]),
+        pltpu.make_async_copy(pgrad, pgrad_out, loc.at[7]),
+        pltpu.make_async_copy(sgrad, sgrad_out, loc.at[8]),
+        pltpu.make_async_copy(igrad, igrad_out, loc.at[9]),
+    ]
+    results[0].start()
+    results[1].start()
     grad_end(0)
     grad_end(1)
+    results[2].start()
     for copy in started[:early]:
         copy.wait_send()
     rs_end(1, igrad)
+    results[3].start()
+    for copy in results:
+        copy.wait()
     for copy in started[early:]:
         copy.wait_send()
 
@@ -418,6 +438,12 @@
     vmem_spec = pl.BlockSpec(memory_space=pltpu.VMEM)
     dma = pltpu.SemaphoreType.DMA
     scratch = [
+        pltpu.VMEM((TOPK, TOK), jnp.int32),
+        pltpu.VMEM((TOPK, TOK), F32),
+        pltpu.VMEM((TOK, D), BF16),
+        pltpu.VMEM((TOK, D), BF16),
+        pltpu.VMEM((1, FF // 8, D), BF16),
+        pltpu.VMEM((TOPK, TOK), F32),
         pltpu.VMEM((2, ROWS, D), BF16),
         pltpu.VMEM((D, NX * FF), BF16),
         pltpu.VMEM((NX * FF, D), BF16),
@@ -451,7 +477,7 @@
         dma((2,)), dma((2,)),
         dma((2, 3)), dma((2, 3)),
         dma((2, 3)), dma((2, 3)),
-        dma((4,)),
+        dma((10,)),
     ]
     results = pl.pallas_call(
         kernel,
@@ -461,8 +487,8 @@
             jax.ShapeDtypeStruct((1, FF // 8, D), BF16),
             jax.ShapeDtypeStruct((TOPK, TOK), F32),
         ),
-        in_specs=[any_spec] * 4 + [vmem_spec] * 2,
-        out_specs=(vmem_spec,) * 4,
+        in_specs=[any_spec] * 6,
+        out_specs=(any_spec,) * 4,
         scratch_shapes=scratch,
         compiler_params=pltpu.CompilerParams(
             collective_id=0, has_side_effects=True, vmem_limit_bytes=60 * 1024 * 1024

time: 100 us -> 99.5 us (level)
  no operation moved by 1% of the time
where the time goes in v5:
time: 99.5 us; the launch traced here: 98.2 us
  Pallas kernels  97.6 us (98%)
    pallas_call x1, Pallas kernels, body(): pl.pallas_call(kernel, out_shape=(jax.ShapeDtypeStruct((TOK, D), BF16), j...  95.7 us

profile of v5, /device:TPU:2, one launch (start us, length us, event | category | flops | bytes accessed | tf_op | source)
XLA Modules:
  0.0 98.2 jit_solution(5029363685587539369)
XLA Ops:
  0.6 95.7 %shard_map.93 = (bf16[128,1024]{1,0:T(8,128)(2,1)}, bf16[128,1024]{1,0:T(8,128)(2,1)}, bf16[1,64,1024]{2,1,0:T(8,128)(2,1)}, f32[8,128]{1,0:T(8,128)}) custom-call(bf16[128,1024]{1,0:T(8,128)(2,1)} %tok_in.1, bf16[128,1024]{1,0:T(8,128)(2,1)} %up_in.1, bf16[1,1024,512]{2,1,0:T(8,128)(2,1)} %w1_in.1, bf16[1,512,1024]{2,1,0:T(8,128)(2,1)} %w2_in.1, ...), custom_call_target="tpu_custom_call" | custom-call | flops 21474836480 | bytes 8388608 | tf_op jit(solution)/shard_map/pallas_call | solution.py:482
  96.3 1.9 %shard_map.94 = (bf16[128,1024]{1,0:T(8,128)(2,1)}, bf16[128,1024]{1,0:T(8,128)(2,1)}, bf16[1,64,1024]{2,1,0:T(8,128)(2,1)}, f32[8,128]{1,0:T(8,128)}) custom-call(bf16[128,1024]{1,0:T(8,128)(2,1)} %get-tuple-element.12.a0, bf16[128,1024]{1,0:T(8,128)(2,1)} %get-tuple-element.13.a1, bf16[1,64,1024]{2,1,0:T(8,128)(2,1)} %get-tuple-element.14.a2, ...), custom_call_target="tpu_custom_call" | custom-call | tf_op jit(solution)/shard_map/pallas_call | solution.py:501

commit v6 on v5

--- a/solution.py
+++ b/solution.py
@@ -372,12 +372,12 @@
     pre_block(0, 4, 2, 4)
     each(wy_relay, 1)
     ag_hop(0, 3)
-    pre_block(4, 3)
+    pre_block(4, 3, 0, 2)
     ag_hop(1, 3, 0)
+    pre_block(4, 3, 2, 4)
+    ag_hop(1, 3, 1)
     each(w_arrive, 1)
     mixed_block(4, 3)
-    ag_hop(1, 3, 1)
-    back_block(0, 4, 0, 1)
     ag_hop(0, 4)
     pre_block(7, 1)
     mixed_block(7, 1)
@@ -394,7 +394,7 @@
     grad_first(0)
     rs_step(1, 3)
     weight_grad(1)
-    back_block(0, 4, 1, 3)
+    back_block(0, 4, 0, 3)
     rs_step(0, 1)
     grad_first(1)
     back_block(0, 4, 3, 4)

time: 99.5 us -> 99.5 us (level)
  no operation moved by 1% of the time
where the time goes in v6:
time: 99.5 us; the launch traced here: 98.2 us
  Pallas kernels  97.6 us (98%)
    pallas_call x1, Pallas kernels, body(): pl.pallas_call(kernel, out_shape=(jax.ShapeDtypeStruct((TOK, D), BF16), j...  95.7 us

profile of v6, /device:TPU:2, one launch (start us, length us, event | category | flops | bytes accessed | tf_op | source)
XLA Modules:
  0.0 98.2 jit_solution(14384268426780874388)
XLA Ops:
  0.6 95.7 %shard_map.93 = (bf16[128,1024]{1,0:T(8,128)(2,1)}, bf16[128,1024]{1,0:T(8,128)(2,1)}, bf16[1,64,1024]{2,1,0:T(8,128)(2,1)}, f32[8,128]{1,0:T(8,128)}) custom-call(bf16[128,1024]{1,0:T(8,128)(2,1)} %tok_in.1, bf16[128,1024]{1,0:T(8,128)(2,1)} %up_in.1, bf16[1,1024,512]{2,1,0:T(8,128)(2,1)} %w1_in.1, bf16[1,512,1024]{2,1,0:T(8,128)(2,1)} %w2_in.1, ...), custom_call_target="tpu_custom_call" | custom-call | flops 21474836480 | bytes 8388608 | tf_op jit(solution)/shard_map/pallas_call | solution.py:482
  96.3 1.9 %shard_map.94 = (bf16[128,1024]{1,0:T(8,128)(2,1)}, bf16[128,1024]{1,0:T(8,128)(2,1)}, bf16[1,64,1024]{2,1,0:T(8,128)(2,1)}, f32[8,128]{1,0:T(8,128)}) custom-call(bf16[128,1024]{1,0:T(8,128)(2,1)} %get-tuple-element.12.a0, bf16[128,1024]{1,0:T(8,128)(2,1)} %get-tuple-element.13.a1, bf16[1,64,1024]{2,1,0:T(8,128)(2,1)} %get-tuple-element.14.a2, ...), custom_call_target="tpu_custom_call" | custom-call | tf_op jit(solution)/shard_map/pallas_call | solution.py:501
